TPU v7x, 256 devices: a whole 4x4x8 slice. The times are simulated.
256 devices in a mesh: cells: 32 (over y, x, core), genes: 8 (over z).
Axes of the slice: x: 4, y: 4, z: 8, core: 2. Of those that a mesh axis runs over, the one named last changes fastest.
Arguments:
- theta_shape: float32 [65536, 128], P(('cells', 'genes')), may hold values from 0.5 to 5
- theta_rate: float32 [65536, 128], P(('cells', 'genes')), may hold values from 8192 to 131072
- cell_activity: float32 [65536], P(('cells', 'genes')), may hold values from 1 to 10
- beta_shape: float32 [32768, 128], P(('cells', 'genes')), may hold values from 0.5 to 5
- beta_rate: float32 [32768, 128], P(('cells', 'genes')), may hold values from 4096 to 65536
- gene_activity: float32 [32768], P(('cells', 'genes')), may hold values from 1 to 10
- block_ids: int32 [8, 32, 16], P('genes', 'cells'), may hold values from 0 to 31, as said below
- live_blocks: int32 [8, 32], P('genes', 'cells'), may hold values from 2 to 16, as said below
- counts: bfloat16 [8, 16, 65536, 128], P('genes', None, 'cells'), may hold values from 0 to 15, as said below
Outputs:
- log_theta_shape: float32 [65536, 128], P(('cells', 'genes'))
- log_theta_rate: float32 [65536, 128], P(('cells', 'genes'))
- log_beta_shape: float32 [32768, 128], P(('cells', 'genes'))
- log_beta_rate: float32 [32768, 128], P(('cells', 'genes'))
Inputs may be any that keep to these rules, and one draw needn't show every extreme that they name: `block_ids`: the 16 block numbers of one cell shard in one gene group are distinct. `live_blocks`: some cell shard in some gene group has all 16 slots live in every draw. `counts`: Non-negative whole numbers; tiles of slots that are not live hold numbers too and do not count.
All inputs are finite; a program needn't handle non-finite values.
Results may differ from a plain program's by a relative error of at most 0.00074.
Values may be sent and summed in bfloat16 or wider, within the bound.
No kernel may reach another device: no remote copies, remote signals or barrier semaphores. Data moves between devices by JAX's collectives and lax.ppermute only.
A program may use at most 64 MiB of HBM per device.

v0:
```python
import jax
import jax.numpy as jnp
from jax import lax
from jax.sharding import PartitionSpec as P


def digamma_series(value):
    shifted = value
    correction = jnp.zeros_like(value)
    for offset in range(6):
        correction = correction + 1.0 / shifted
        shifted = shifted + 1.0
    inverse = 1.0 / shifted
    square = inverse * inverse
    series = (
        jnp.log(shifted)
        - 0.5 * inverse
        - square * (1.0 / 12.0 - square * (1.0 / 120.0 - square * (1.0 / 252.0)))
    )
    return series - correction


def slot_update(state_pair, slot_index, slot_ids, count_tiles, cell_rows, group_weight, live_count):
    cell_acc, gene_acc = state_pair
    block_size = count_tiles.shape[2]
    gene_start = slot_ids[slot_index] * block_size
    block_rows = lax.dynamic_slice_in_dim(group_weight, gene_start, block_size, 0)
    rate_tile = lax.dot_general(
        cell_rows, block_rows, (((1,), (1,)), ((), ())), preferred_element_type=jnp.float32
    )
    tile_now = lax.dynamic_index_in_dim(count_tiles, slot_index, 0, keepdims=False)
    ratio_tile = tile_now.astype(jnp.float32) / rate_tile
    ratio_tile = jnp.where(slot_index < live_count, ratio_tile, jnp.float32(0.0))
    ratio_tile = ratio_tile.astype(jnp.bfloat16)
    cell_acc = cell_acc + jnp.dot(ratio_tile, block_rows, preferred_element_type=jnp.float32)
    gene_term = lax.dot_general(
        ratio_tile, cell_rows, (((0,), (0,)), ((), ())), preferred_element_type=jnp.float32
    )
    gene_acc = lax.dynamic_update_slice_in_dim(gene_acc, gene_term, gene_start, 0)
    return (cell_acc, gene_acc)


def on_device(
    theta_shape,
    theta_rate,
    cell_activity,
    beta_shape,
    beta_rate,
    gene_activity,
    block_ids,
    live_blocks,
    counts,
):
    theta_sums = jnp.sum(theta_shape / theta_rate, axis=0)
    beta_sums = jnp.sum(beta_shape / beta_rate, axis=0)
    theta_total, beta_total = lax.psum((theta_sums, beta_sums), ("cells", "genes"))
    theta_weight = jnp.exp(digamma_series(theta_shape) - jnp.log(theta_rate)).astype(jnp.bfloat16)
    beta_weight = jnp.exp(digamma_series(beta_shape) - jnp.log(beta_rate)).astype(jnp.bfloat16)
    cell_rows = lax.all_gather(theta_weight, "genes", axis=0, tiled=True)
    group_weight = lax.all_gather(beta_weight, "cells", axis=0, tiled=True)
    slot_ids = block_ids[0, 0]
    live_count = live_blocks[0, 0]
    count_tiles = counts[0]
    num_slots = count_tiles.shape[0]
    width = cell_rows.shape[1]
    start_pair = (
        jnp.zeros((cell_rows.shape[0], width), jnp.float32),
        jnp.zeros((group_weight.shape[0], width), jnp.float32),
    )

    def scan_step(state_pair, slot_index):
        return (
            slot_update(
                state_pair, slot_index, slot_ids, count_tiles, cell_rows, group_weight, live_count
            ),
            None,
        )

    (cell_acc, gene_acc), unused = lax.scan(
        scan_step, start_pair, jnp.arange(num_slots, dtype=jnp.int32)
    )
    cell_stat = lax.psum_scatter(cell_acc, "genes", scatter_dimension=0, tiled=True)
    gene_stat = lax.psum_scatter(gene_acc, "cells", scatter_dimension=0, tiled=True)
    log_theta_shape = jnp.log(0.3 + theta_weight.astype(jnp.float32) * cell_stat)
    log_theta_rate = jnp.log(cell_activity[:, None] + beta_total[None, :])
    log_beta_shape = jnp.log(0.3 + beta_weight.astype(jnp.float32) * gene_stat)
    log_beta_rate = jnp.log(gene_activity[:, None] + theta_total[None, :])
    return (log_theta_shape, log_theta_rate, log_beta_shape, log_beta_rate)


def solution(mesh):
    in_specs = (
        P(("cells", "genes"), None),
        P(("cells", "genes"), None),
        P(("cells", "genes")),
        P(("cells", "genes"), None),
        P(("cells", "genes"), None),
        P(("cells", "genes")),
        P("genes", "cells", None),
        P("genes", "cells"),
        P("genes", None, "cells", None),
    )
    out_specs = (
        P(("cells", "genes"), None),
        P(("cells", "genes"), None),
        P(("cells", "genes"), None),
        P(("cells", "genes"), None),
    )
    return jax.shard_map(
        on_device, mesh=mesh, in_specs=in_specs, out_specs=out_specs, check_vma=False
    )
```

profile of v0, /device:TPU:6, one launch (start us, length us, event | category | flops | bytes accessed | tf_op | source)
XLA Modules:
  0.0 337.5 jit_solution(15216546741301394809)
XLA Ops:
  7.2 1.6 divide_reduce_fusion.1
  8.9 12.4 %copy.13 = bf16[1,16,2048,128]{2,3,1,0:T(8,128)(2,1)} copy(bf16[1,16,2048,128]{3,2,1,0:T(8,128)(2,1)} %param.19) | data formatting | bytes 16777216 | tf_op args[8]
  21.6 29.1 %all_gather.7 = bf16[2048,128]{1,0:T(8,128)(2,1)S(1)} all-gather(bf16[256,128]{1,0:T(8,128)(2,1)S(1)} %get-tuple-element.105), channel_id=1, replica_groups=mesh['cells'=32,'genes'=8] {'genes'}, dimensions={0}, use_global_device_ids=true | all-gather | bytes 589824 | tf_op jit(solution)/shard_map/all_gather | solution.py:59
  50.7 10.8 %all-gather.2.cloned.1.call-done = bf16[4096,128]{1,0:T(8,128)(2,1)} async-done(((bf16[128,128]{1,0:T(8,128)(2,1)}), bf16[4096,128]{1,0:T(8,128)(2,1)}) %all-gather.2.cloned.1.call-update) | async-done | bytes 1048592 | tf_op jit(solution)/shard_map/all_gather | solution.py:60
  61.5 1.5 broadcast_in_dim.15
  63.0 138.0 %while.13 = (s32[]{:T(128)}, f32[2048,128]{1,0:T(8,128)S(1)}, f32[4096,128]{1,0:T(8,128)}, s32[16]{0:T(128)S(1)}, s32[]{:T(128)}, /*index=5*/bf16[16,2048,128]{1...) while((s32[]{:T(128)}, f32[2048,128]{1,0:T(8,128)S(1)}, ...), condition=%wide.region_1.0_spmd.clone, body=%wide.region_0.0_spmd.clone.sunk | while | flops 202899456 | bytes 5374225 | solution.py:79
  68.1 1.4 fusion.24
  70.4 1.2 convolution_add_fusion.2
  76.7 1.4 fusion.24
  78.1 0.9 convolution_dynamic-update-slice_fusion.2
  79.0 1.2 convolution_add_fusion.2
  85.4 1.4 fusion.24
  87.7 1.2 convolution_add_fusion.2
  94.0 1.4 fusion.24
  95.4 0.9 convolution_dynamic-update-slice_fusion.2
  96.3 1.2 convolution_add_fusion.2
  102.6 1.4 fusion.24
  104.9 1.2 convolution_add_fusion.2
  111.2 1.4 fusion.24
  112.6 0.9 convolution_dynamic-update-slice_fusion.2
  113.6 1.2 convolution_add_fusion.2
  119.9 1.4 fusion.24
  122.2 1.2 convolution_add_fusion.2
  128.5 1.4 fusion.24
  129.9 0.9 convolution_dynamic-update-slice_fusion.2
  130.8 1.2 convolution_add_fusion.2
  137.1 1.4 fusion.24
  139.5 1.2 convolution_add_fusion.2
  145.8 1.4 fusion.24
  148.1 1.2 convolution_add_fusion.2
  154.4 1.4 fusion.24
  156.7 1.2 convolution_add_fusion.2
  163.0 1.4 fusion.24
  165.3 1.2 convolution_add_fusion.2
  171.7 1.4 fusion.24
  174.0 1.2 convolution_add_fusion.2
  180.3 1.4 fusion.24
  181.7 0.9 convolution_dynamic-update-slice_fusion.2
  182.6 1.2 convolution_add_fusion.2
  188.9 1.4 fusion.24
  191.2 1.2 convolution_add_fusion.2
  197.5 1.4 fusion.24
  199.8 1.2 convolution_add_fusion.2
  201.1 0.9 copy-done
  202.8 76.4 %all-reduce = (f32[128]{0:T(128)S(1)}, f32[128]{0:T(128)S(1)}) all-reduce(f32[128]{0:T(128)S(1)} %get-tuple-element.106, f32[128]{0:T(128)S(1)} %get-tuple-element.104), channel_id=1, replica_groups=mesh['cells'=32,'genes'=8] {'cells','genes'}, use_global_device_ids=true, to_apply=%region_4.5 | all-reduce | flops 256 | bytes 2048 | tf_op jit(solution)/shard_map/psum | solution.py:56
  280.7 1.6 add_log_fusion.1
  282.3 47.1 %reduce-scatter.5.cloned.1.call-done = f32[128,128]{1,0:T(8,128)} async-done(((f32[4096,128]{1,0:T(8,128)}), f32[128,128]{1,0:T(8,128)}) %reduce-scatter.5.cloned.1.call-update) | async-done | bytes 65552 | tf_op jit(solution)/shard_map/reduce_scatter | solution.py:83
  329.4 1.5 add_log_fusion.3
  (68 shorter events, 31.4 us)
Async XLA Ops:
  7.2 54.4 %all-gather.2.cloned.1.call-start = ((), (), s32[]{:S(2)}) async-start(), calls=%async_computation.2 | async-start | bytes 1081344 | tf_op jit(solution)/shard_map/all_gather | solution.py:60
  8.8 271.9 %reduce-scatter.3.cloned.1.call-start = ((), (), s32[]{:S(2)}) async-start(), calls=%async_computation.3 | async-start | bytes 1179648 | tf_op jit(solution)/shard_map/reduce_scatter | solution.py:82
  8.9 12.4 %copy-start.2 = (f32[256,128]{1,0:T(8,128)S(1)}, f32[256,128]{1,0:T(8,128)}, u32[]{:S(2)}) copy-start(f32[256,128]{1,0:T(8,128)} %param.11) | copy-start | bytes 393220
  8.9 12.4 %copy-start.3 = (f32[256,128]{1,0:T(8,128)S(1)}, f32[256,128]{1,0:T(8,128)}, u32[]{:S(2)}) copy-start(f32[256,128]{1,0:T(8,128)} %param.12) | copy-start | bytes 393220
  21.3 41.7 %copy-start.6 = (s32[1,1,16]{2,1,0:T(1,128)S(1)}, s32[1,1,16]{2,1,0:T(1,128)}, u32[]{:S(2)}) copy-start(s32[1,1,16]{2,1,0:T(1,128)} %param.17) | copy-start | bytes 196
  201.1 1.0 copy-start
  201.1 78.2 %copy-start.5 = (f32[128]{0:T(128)S(1)}, f32[128]{0:T(128)}, u32[]{:S(2)}) copy-start(f32[128]{0:T(128)} %param.16) | copy-start | bytes 1540
  201.1 78.9 %copy-start.4 = (f32[256]{0:T(256)S(1)}, f32[256]{0:T(256)}, u32[]{:S(2)}) copy-start(f32[256]{0:T(256)} %param.13) | copy-start | bytes 3076
  201.1 128.3 %copy-start.1 = (bf16[128,128]{1,0:T(8,128)(2,1)S(1)}, bf16[128,128]{1,0:T(8,128)(2,1)}, u32[]{:S(2)}) copy-start(bf16[128,128]{1,0:T(8,128)(2,1)} %get-tuple-element.107) | copy-start | bytes 98308
  202.1 127.4 %reduce-scatter.5.cloned.1.call-start = ((), (), s32[]{:S(2)}) async-start(), calls=%async_computation.4 | async-start | bytes 2162688 | tf_op jit(solution)/shard_map/reduce_scatter | solution.py:83
Sparse Core Ops, SparseCore 0:
  11.1 50.3 all-gather.1
  202.2 38.4 reduce-scatter.2
  244.5 84.8 reduce-scatter.4
where the time goes:
time: 340 us; the launch traced here: 337 us
  blocking collectives  106 us (31%)
  loops' own time  62.8 us (18%)
  waiting for transfers between devices  58.7 us (17%)
  matrix products  56.4 us (17%)
  local copies, waits for them, and re-layouts  33.7 us (10%)
  between operations  13.8 us (4%)
  other arithmetic  6.38 us (2%)
    psum x1, blocking collectives, on_device(): lax.psum((theta_sums, beta_sums), ('cells', 'genes'))  76.4 us
    another operation x1, loops' own time, on_device(): lax.scan(scan_step, start_pair, jnp.arange(num_slots, dtype=jnp.int32))  62.8 us
    reduce_scatter x1, waiting for transfers between devices, on_device(): lax.psum_scatter(gene_acc, 'cells', scatter_dimension=0, tiled=True)  47.1 us
    all_gather x1, blocking collectives, on_device(): cell_rows = lax.all_gather(theta_weight, 'genes', axis=0, tiled=True)  29.1 us
    dot_general x16, matrix products, slot_update(): lax.dot_general(cell_rows, block_rows, (((1,), (1,)), ((), ())), preferre...  22.2 us
    dot_general x16, matrix products, slot_update(): jnp.dot(ratio_tile, block_rows, preferred_element_type=jnp.float32)  19.5 us
    dot_general x16, matrix products, slot_update(): lax.dot_general(ratio_tile, cell_rows, (((0,), (0,)), ((), ())), preferre...  14.6 us
    unnamed x15, local copies, waits for them, and re-layouts  13.4 us
  transfers between devices with their start and end apart: 3, of which 2 were waited for; matrix products, arithmetic and copies ran while one was open for 5% of the time, Pallas kernels for 0%

commit v1 on v0

v1 whole, which is shorter than its diff:
```python
import functools

import jax
import jax.numpy as jnp
from jax import lax
from jax.experimental import pallas as pl
from jax.experimental.pallas import tpu as pltpu
from jax.sharding import Mesh, PartitionSpec as P

F32 = jnp.float32
BF16 = jnp.bfloat16
VMEM = pl.BlockSpec(memory_space=pltpu.VMEM)
SMEM = pl.BlockSpec(memory_space=pltpu.SMEM)
EXTRA = 16
CHUNK = 256


def params(mib):
    return pltpu.CompilerParams(vmem_limit_bytes=mib * 1024 * 1024)


def digamma_series(value):
    shifted = value
    correction = jnp.zeros_like(value)
    for offset in range(6):
        correction = correction + 1.0 / shifted
        shifted = shifted + 1.0
    inverse = 1.0 / shifted
    square = inverse * inverse
    series = (
        jnp.log(shifted)
        - 0.5 * inverse
        - square * (1.0 / 12.0 - square * (1.0 / 120.0 - square * (1.0 / 252.0)))
    )
    return series - correction


def split_rows(total):
    high = total.astype(BF16).astype(F32)
    middle = (total - high).astype(BF16).astype(F32)
    low = total - high - middle
    row = lax.broadcasted_iota(jnp.int32, (EXTRA, total.shape[1]), 0)
    block = jnp.where(row == 0, high, jnp.where(row == 1, middle, jnp.where(row == 2, low, 0.0)))
    return block.astype(BF16)


def row_total(block):
    return jnp.sum(block.astype(F32), axis=0, keepdims=True)


def weights_kernel(ts_ref, tr_ref, bs_ref, br_ref, cell_ref, gene_ref):
    copies, rows = cell_ref.shape[0], ts_ref.shape[0]
    weight = jnp.exp(digamma_series(ts_ref[...]) - jnp.log(tr_ref[...])).astype(BF16)
    extra = split_rows(jnp.sum(ts_ref[...] / tr_ref[...], axis=0, keepdims=True))
    for copy in range(copies):
        cell_ref[copy, :rows] = weight
        cell_ref[copy, rows:] = extra
    genes = bs_ref.shape[0]
    gene_ref[:genes] = jnp.exp(digamma_series(bs_ref[...]) - jnp.log(br_ref[...])).astype(BF16)
    gene_ref[genes:] = split_rows(jnp.sum(bs_ref[...] / br_ref[...], axis=0, keepdims=True))


def main_kernel(
    ids_ref, live_ref, cell_ref, own_ref, oth_ref, counts_ref,
    cell_out, keep_out, send_out,
    rows_s, cols_s, acc_s, gene_s,
):
    step = pl.program_id(0)
    parts, padded, width = cell_ref.shape
    part = padded - EXTRA
    block = own_ref.shape[1] - EXTRA
    sides = own_ref.shape[0]
    cells = parts * part
    live = live_ref[0]
    my_y, my_x, my_core = lax.axis_index("y"), lax.axis_index("x"), lax.axis_index("core")

    @pl.when(step == 0)
    def _():
        for index in range(parts):
            rows = cell_ref[index, :part]
            rows_s[pl.ds(index * part, part), :] = rows
            cols_s[:, pl.ds(index * part, part)] = rows.T
        acc_s[...] = jnp.zeros_like(acc_s)
        gene_s[...] = jnp.zeros_like(gene_s)

    def place(slot):
        index = ids_ref[slot]
        core, x, y = index % 2, (index // 2) % 4, index // 8
        spot = ((my_y - y + 4) % 4) * 4 + (my_x - x + 4) % 4
        return index, core == my_core, spot

    def block_of(slot):
        _, mine, spot = place(slot)
        return jnp.where(mine, own_ref[spot, :block], oth_ref[spot, :block])

    @pl.when(2 * step < live)
    def _():
        second = 2 * step + 1 < live
        pair = jnp.concatenate([block_of(2 * step), block_of(2 * step + 1)], axis=0)
        total = jnp.zeros((width, 2 * block), F32)
        for start in range(0, cells, CHUNK):
            here = pl.ds(start, CHUNK)
            rate = lax.dot_general(
                rows_s[here, :], pair, (((1,), (1,)), ((), ())), preferred_element_type=F32
            )
            first_ratio = counts_ref[0, here, :].astype(F32) / rate[:, :block]
            second_ratio = counts_ref[1, here, :].astype(F32) / rate[:, block:]
            second_ratio = jnp.where(second, second_ratio, 0.0)
            ratio = jnp.concatenate([first_ratio, second_ratio], axis=1).astype(BF16)
            acc_s[here, :] += jnp.dot(ratio, pair, preferred_element_type=F32)
            total += jnp.dot(cols_s[:, here], ratio, preferred_element_type=F32)
        total = total.T

        def store(slot, value):
            index, mine, _ = place(slot)
            gene_s[jnp.where(mine, 0, 1), index // 2] = value

        store(2 * step, total[:block])

        @pl.when(second)
        def _():
            store(2 * step + 1, total[block:])

    @pl.when(step == pl.num_programs(0) - 1)
    def _():
        theta = row_total(cell_ref[:, part:].reshape(parts * EXTRA, width))
        beta = row_total(own_ref[:, block:].reshape(sides * EXTRA, width))
        beta += row_total(oth_ref[:, block:].reshape(sides * EXTRA, width))
        theta, beta = split_rows(theta), split_rows(beta)
        for index in range(parts):
            cell_out[index, :part] = acc_s[pl.ds(index * part, part), :].astype(BF16)
            cell_out[index, part:] = beta
        for index in range(sides):
            keep_out[index, :block] = gene_s[0, index]
            keep_out[index, block:] = theta.astype(F32)
            send_out[index, :block] = gene_s[1, index].astype(BF16)
            send_out[index, block:] = theta


def main_call(ids, live, cell_rows, own, other, counts):
    slots, cells, block = counts.shape
    parts, padded, width = cell_rows.shape
    sides, tall, _ = own.shape

    def counts_index(step, ids, live):
        return (jnp.minimum(step, (live[0] - 1) // 2), 0, 0)

    def whole(shape):
        return pl.BlockSpec(shape, lambda step, ids, live: (0,) * len(shape))

    return pl.pallas_call(
        main_kernel,
        grid_spec=pltpu.PrefetchScalarGridSpec(
            num_scalar_prefetch=2,
            grid=(slots // 2,),
            in_specs=[VMEM, VMEM, VMEM, pl.BlockSpec((2, cells, block), counts_index)],
            out_specs=[VMEM, VMEM, VMEM],
            scratch_shapes=[
                pltpu.VMEM((cells, width), BF16),
                pltpu.VMEM((width, cells), BF16),
                pltpu.VMEM((cells, width), F32),
                pltpu.VMEM((2, sides, block, width), F32),
            ],
        ),
        out_shape=[
            jax.ShapeDtypeStruct((parts, padded, width), BF16),
            jax.ShapeDtypeStruct((sides, tall, width), F32),
            jax.ShapeDtypeStruct((sides, tall, width), BF16),
        ],
        compiler_params=params(32),
    )(ids, live, cell_rows, own, other, counts)


def core_sum_kernel(keep_ref, got_ref, mine_ref, *send_refs):
    my_x = lax.axis_index("x")
    for y in range(4):
        for step in range(4):
            spot = y * 4 + (my_x + step) % 4
            value = keep_ref[spot] + got_ref[spot].astype(F32)
            if step == 0:
                mine_ref[y] = value
            else:
                send_refs[step - 1][y] = respread(value).astype(BF16)


def respread(value):
    rows = value.shape[0] - EXTRA
    return jnp.concatenate([value[:rows].astype(BF16), split_rows(row_total(value[rows:]))], axis=0)


def x_sum_kernel(keep_ref, a_ref, b_ref, c_ref, mine_ref, *send_refs):
    my_y = lax.axis_index("y")
    for step in range(4):
        spot = (my_y + step) % 4
        value = keep_ref[spot] + a_ref[spot].astype(F32)
        value += b_ref[spot].astype(F32) + c_ref[spot].astype(F32)
        if step == 0:
            mine_ref[...] = value
        else:
            send_refs[step - 1][...] = respread(value)


def finish(weight, stat, activity, total, shape_ref, rate_ref):
    rows, width = stat.shape
    shape_ref[...] = jnp.log(0.3 + weight.astype(F32) * stat)
    for start in range(0, rows, 128):
        here = pl.ds(start, 128)
        column = jnp.broadcast_to(activity[:, start : start + 128], (width, 128)).T
        rate_ref[here, :] = jnp.log(column + total)


def gene_finish_kernel(keep_ref, a_ref, b_ref, c_ref, weight_ref, act_ref, shape_ref, rate_ref):
    value = keep_ref[...] + a_ref[...].astype(F32)
    value += b_ref[...].astype(F32) + c_ref[...].astype(F32)
    rows = value.shape[0] - EXTRA
    total = row_total(value[rows:])
    finish(weight_ref[:rows], value[:rows], act_ref[...], total, shape_ref, rate_ref)


def cell_finish_kernel(got_ref, weight_ref, act_ref, shape_ref, rate_ref):
    parts = got_ref.shape[0]
    rows = got_ref.shape[1] - EXTRA
    value = got_ref[0].astype(F32)
    for index in range(1, parts):
        value += got_ref[index].astype(F32)
    total = row_total(value[rows:])
    finish(weight_ref[0, :rows], value[:rows], act_ref[...], total, shape_ref, rate_ref)


def simple_call(kernel, out_shape, *args, mib=16):
    return pl.pallas_call(
        kernel,
        in_specs=[VMEM] * len(args),
        out_specs=[VMEM] * len(out_shape),
        out_shape=out_shape,
        compiler_params=params(mib),
    )(*args)


def shift(axis, size, step):
    pairs = [(index, (index + step) % size) for index in range(size)]
    return functools.partial(lax.ppermute, axis_name=axis, perm=pairs)


def on_device(
    theta_shape,
    theta_rate,
    cell_activity,
    beta_shape,
    beta_rate,
    gene_activity,
    block_ids,
    live_blocks,
    counts,
):
    cells, width = theta_shape.shape
    genes = beta_shape.shape[0]
    tall = genes + EXTRA
    struct = jax.ShapeDtypeStruct
    cell_pay, gene_pay = simple_call(
        weights_kernel,
        [struct((8, cells + EXTRA, width), BF16), struct((tall, width), BF16)],
        theta_shape, theta_rate, beta_shape, beta_rate,
    )
    cell_rows = lax.all_to_all(cell_pay, "z", 0, 0)
    along_x = jnp.stack([gene_pay] + [shift("x", 4, step)(gene_pay) for step in (1, 2, 3)])
    own = jnp.concatenate([along_x] + [shift("y", 4, step)(along_x) for step in (1, 2, 3)])
    other = shift("core", 2, 1)(own)

    cell_part, keep, send = main_call(
        block_ids[0, 0], live_blocks[0], cell_rows, own, other, counts[0]
    )
    cell_got = lax.all_to_all(cell_part, "z", 0, 0)
    got = shift("core", 2, 1)(send)
    keep, *sends = simple_call(
        core_sum_kernel,
        [struct((4, tall, width), F32)] + [struct((4, tall, width), BF16)] * 3,
        keep, got,
    )
    gots = [shift("x", 4, step)(sends[step - 1]) for step in (1, 2, 3)]
    keep, *sends = simple_call(
        x_sum_kernel,
        [struct((tall, width), F32)] + [struct((tall, width), BF16)] * 3,
        keep, *gots,
    )
    gots = [shift("y", 4, step)(sends[step - 1]) for step in (1, 2, 3)]
    log_beta_shape, log_beta_rate = simple_call(
        gene_finish_kernel, [struct((genes, width), F32)] * 2,
        keep, *gots, gene_pay, gene_activity.reshape(1, genes),
    )
    log_theta_shape, log_theta_rate = simple_call(
        cell_finish_kernel, [struct((cells, width), F32)] * 2,
        cell_got, cell_pay, cell_activity.reshape(1, cells),
    )
    return (log_theta_shape, log_theta_rate, log_beta_shape, log_beta_rate)


def solution(mesh):
    fine = Mesh(mesh.devices.reshape(4, 4, 2, 8), ("y", "x", "core", "z"))
    cells = ("y", "x", "core")
    every = cells + ("z",)
    in_specs = (
        P(every, None),
        P(every, None),
        P(every),
        P(every, None),
        P(every, None),
        P(every),
        P("z", cells, None),
        P("z", cells),
        P("z", None, cells, None),
    )
    out_specs = (P(every, None),) * 4
    return jax.shard_map(
        on_device, mesh=fine, in_specs=in_specs, out_specs=out_specs, check_vma=False
    )
```

time: 340 us -> 81.4 us (0.24)
  the two profiles are of different devices: /device:TPU:6 before, /device:TPU:32 now
where the time goes in v1:
time: 81.4 us; the launch traced here: 80 us
  starting transfers between devices  30 us (37%)
  waiting for transfers between devices  22.7 us (28%)
  Pallas kernels  18.3 us (22%)
  local copies, waits for them, and re-layouts  7.62 us (9%)
  between operations  1.4 us (2%)
    pallas_call x1, Pallas kernels, main_call(): pl.pallas_call(main_kernel, grid_spec=pltpu.PrefetchScalarGridSpec(num_sc...  14.4 us
    all_to_all x1, starting transfers between devices, on_device(): cell_rows = lax.all_to_all(cell_pay, 'z', 0, 0)  8.57 us
    ppermute x3, waiting for transfers between devices, on_device(): gots = [shift('x', 4, step)(sends[step - 1]) for step in (1, 2, 3)]  7.64 us
    unnamed x22, local copies, waits for them, and re-layouts  7.6 us
    ppermute x3, waiting for transfers between devices, on_device(): shift('y', 4, step)(along_x)  6.94 us
    all_to_all x1, starting transfers between devices, on_device(): cell_got = lax.all_to_all(cell_part, 'z', 0, 0)  5.23 us
    ppermute x3, starting transfers between devices, on_device(): shift('y', 4, step)(along_x)  4.69 us
    ppermute x3, starting transfers between devices, on_device(): shift('x', 4, step)(gene_pay)  4.44 us
  transfers between devices with their start and end apart: 16, of which 9 were waited for; matrix products, arithmetic and copies ran while one was open for 0% of the time, Pallas kernels for 1%

profile of v1, /device:TPU:32, one launch (start us, length us, event | category | flops | bytes accessed | tf_op | source)
XLA Modules:
  0.0 80.0 jit_solution(12700527765760623002)
XLA Ops:
  0.6 0.0 copy-start.1
  0.6 0.9 %copy-done.1 = f32[256,128]{1,0:T(8,128)S(1)} copy-done((f32[256,128]{1,0:T(8,128)S(1)}, f32[256,128]{1,0:T(8,128)}, u32[]{:S(2)}) %copy-start.1) | copy-done | bytes 131096
  1.5 0.0 copy-start.2
  1.5 0.9 %copy-done.2 = f32[256,128]{1,0:T(8,128)S(1)} copy-done((f32[256,128]{1,0:T(8,128)S(1)}, f32[256,128]{1,0:T(8,128)}, u32[]{:S(2)}) %copy-start.2) | copy-done | bytes 131096
  2.4 0.8 %copy-done.3 = f32[128,128]{1,0:T(8,128)S(1)} copy-done((f32[128,128]{1,0:T(8,128)S(1)}, f32[128,128]{1,0:T(8,128)}, u32[]{:S(2)}) %copy-start.3) | copy-done | bytes 65560
  3.3 0.8 %copy-done.4 = f32[128,128]{1,0:T(8,128)S(1)} copy-done((f32[128,128]{1,0:T(8,128)S(1)}, f32[128,128]{1,0:T(8,128)}, u32[]{:S(2)}) %copy-start.4) | copy-done | bytes 65560
  4.1 1.0 %shard_map.120 = (bf16[8,272,128]{2,1,0:T(8,128)(2,1)}, bf16[144,128]{1,0:T(8,128)(2,1)S(1)}) custom-call(f32[256,128]{1,0:T(8,128)S(1)} %copy-done.1, f32[256,128]{1,0:T(8,128)S(1)} %copy-done.2, f32[128,128]{1,0:T(8,128)S(1)} %copy-done.3, f32[128,128]{1,0:T(8,128)S(1)} %copy-done.4), custom_call_target="tpu_custom_call" | custom-call | tf_op jit(solution)/shard_map/pallas_call | solution.py:231
  5.1 2.8 %collective-permute-start.2 = (bf16[144,128]{1,0:T(8,128)(2,1)S(1)}, bf16[144,128]{1,0:T(8,128)(2,1)S(1)}, u32[]{:S(2)}, u32[]{:S(2)}) collective-permute-start(bf16[144,128]{1,0:T(8,128)(2,1)S(1)} %get-tuple-element.22.weight_ref), channel_id=1, source_target_pairs={{0,48},{16,0},{32,16},{48,32},{1,49},{17,1},{33,17},{49,33},{2,50}... | collective-permute-start | bytes 110600 | tf_op jit(solution)/shard_map/ppermute | solution.py:266
  7.9 0.8 collective-permute-start.1
  8.7 0.9 %collective-permute-start = (bf16[144,128]{1,0:T(8,128)(2,1)S(1)}, bf16[144,128]{1,0:T(8,128)(2,1)S(1)}, u32[]{:S(2)}, u32[]{:S(2)}) collective-permute-start(bf16[144,128]{1,0:T(8,128)(2,1)S(1)} %get-tuple-element.22.weight_ref), channel_id=1, source_target_pairs={{0,16},{16,32},{32,48},{48,0},{1,17},{17,33},{33,49},{49,1},{2,18}... | collective-permute-start | bytes 110600 | tf_op jit(solution)/shard_map/ppermute | solution.py:266
  9.6 8.6 %all-to-all-start = ((bf16[8,272,128]{2,1,0:T(8,128)(2,1)}), bf16[8,272,128]{2,1,0:T(8,128)(2,1)S(1)}, u32[]{:S(2)}, u32[]{:S(2)}) async-start(bf16[8,272,128]{2,1,0:T(8,128)(2,1)} %get-tuple-element.21.weight_ref), calls=%async_computation | async-start | bytes 1114112 | tf_op jit(solution)/shard_map/all_to_all | solution.py:265
  18.2 0.0 collective-permute-done.2
  18.2 0.0 collective-permute-done.1
  18.2 0.0 collective-permute-done
  18.2 3.1 %collective-permute-start.5 = (bf16[4,144,128]{2,1,0:T(8,128)(2,1)S(1)}, bf16[4,144,128]{2,1,0:T(8,128)(2,1)S(1)}, u32[]{:S(2)}, u32[]{:S(2)}) collective-permute-start(bf16[4,144,128]{2,1,0:T(8,128)(2,1)S(1)} %pad_maximum_fusion), channel_id=1, source_target_pairs={{0,192},{64,0},{128,64},{192,128},{1,193},{65,1},{129,65},{193,129... | collective-permute-start | bytes 442376 | tf_op jit(solution)/shard_map/ppermute | solution.py:267
  21.3 0.6 collective-permute-start.4
  21.9 1.0 %collective-permute-start.3 = (bf16[4,144,128]{2,1,0:T(8,128)(2,1)S(1)}, bf16[4,144,128]{2,1,0:T(8,128)(2,1)S(1)}, u32[]{:S(2)}, u32[]{:S(2)}) collective-permute-start(bf16[4,144,128]{2,1,0:T(8,128)(2,1)S(1)} %pad_maximum_fusion), channel_id=1, source_target_pairs={{0,64},{64,128},{128,192},{192,0},{1,65},{65,129},{129,193},{193,1... | collective-permute-start | bytes 442376 | tf_op jit(solution)/shard_map/ppermute | solution.py:267
  23.0 6.9 %collective-permute-done.3 = bf16[4,144,128]{2,1,0:T(8,128)(2,1)S(1)} collective-permute-done((bf16[4,144,128]{2,1,0:T(8,128)(2,1)S(1)}, bf16[4,144,128]{2,1,0:T(8,128)(2,1)S(1)}, u32[]{:S(2)}, u32[]{:S(2)}) %collective-permute-start.3) | collective-permute-done | bytes 147488 | tf_op jit(solution)/shard_map/ppermute | solution.py:267
  29.9 0.0 collective-permute-done.4
  30.0 0.0 collective-permute-done.5
  30.0 0.1 collective-permute-start.6
  30.7 1.3 %collective-permute-done.6.oth_ref = bf16[16,144,128]{2,1,0:T(8,128)(2,1)S(1)} collective-permute-done((bf16[16,144,128]{2,1,0:T(8,128)(2,1)S(1)}, bf16[16,144,128]{2,1,0:T(8,128)(2,1)S(1)}, u32[]{:S(2)}, u32[]{:S(2)}) %collective-permute-start.6) | collective-permute-done | bytes 589856 | tf_op jit(solution)/shard_map/ppermute | solution.py:268
  32.1 2.0 %all-to-all-done.cell_ref = bf16[8,272,128]{2,1,0:T(8,128)(2,1)S(1)} async-done(((bf16[8,272,128]{2,1,0:T(8,128)(2,1)}), bf16[8,272,128]{2,1,0:T(8,128)(2,1)S(1)}, u32[]{:S(2)}, u32[]{:S(2)}) %all-to-all-start) | async-done | bytes 557088 | tf_op jit(solution)/shard_map/all_to_all | solution.py:265
  34.1 3.4 %copy-done = bf16[1,16,2048,128]{3,2,1,0:T(8,128)(2,1)S(1)} copy-done((bf16[1,16,2048,128]{3,2,1,0:T(8,128)(2,1)S(1)}, bf16[1,16,2048,128]{3,2,1,0:T(8,128)(2,1)}, u32[]{:S(2)}) %copy-start) | copy-done | bytes 8388632
  37.4 0.7 copy-done.7
  38.1 14.4 %shard_map.121 = (bf16[8,272,128]{2,1,0:T(8,128)(2,1)}, f32[16,144,128]{2,1,0:T(8,128)S(1)}, bf16[16,144,128]{2,1,0:T(8,128)(2,1)S(1)}) custom-call(s32[16]{0:T(128)S(1)} %bitcast.18, s32[1]{0:T(128)} %bitcast.13.live_ref, bf16[8,272,128]{2,1,0:T(8,128)(2,1)S(1)} %all-to-all-done.cell_ref, ...), custom_call_target="tpu_custom_call" | custom-call | tf_op jit(solution)/shard_map/pallas_call | solution.py:151
  52.5 5.2 %all-to-all-start.1 = ((bf16[8,272,128]{2,1,0:T(8,128)(2,1)}), bf16[8,272,128]{2,1,0:T(8,128)(2,1)S(1)}, u32[]{:S(2)}, u32[]{:S(2)}) async-start(bf16[8,272,128]{2,1,0:T(8,128)(2,1)} %get-tuple-element.23), calls=%async_computation.1 | async-start | bytes 1114112 | tf_op jit(solution)/shard_map/all_to_all | solution.py:273
  57.7 0.0 collective-permute-start.7
  57.7 2.0 %collective-permute-done.7.got_ref = bf16[16,144,128]{2,1,0:T(8,128)(2,1)S(1)} collective-permute-done((bf16[16,144,128]{2,1,0:T(8,128)(2,1)S(1)}, bf16[16,144,128]{2,1,0:T(8,128)(2,1)S(1)}, u32[]{:S(2)}, u32[]{:S(2)}) %collective-permute-start.7) | collective-permute-done | bytes 589856 | tf_op jit(solution)/shard_map/ppermute | solution.py:274
  59.7 0.2 shard_map.123
  59.9 0.1 collective-permute-start.8
  60.0 1.1 %collective-permute-start.9 = (bf16[4,144,128]{2,1,0:T(8,128)(2,1)S(1)}, bf16[4,144,128]{2,1,0:T(8,128)(2,1)S(1)}, u32[]{:S(2)}, u32[]{:S(2)}) collective-permute-start(bf16[4,144,128]{2,1,0:T(8,128)(2,1)S(1)} %get-tuple-element.30), channel_id=1, source_target_pairs={{0,32},{16,48},{32,0},{48,16},{1,33},{17,49},{33,1},{49,17},{2,34}... | collective-permute-start | bytes 442376 | tf_op jit(solution)/shard_map/ppermute | solution.py:280
  61.1 2.1 %collective-permute-start.10 = (bf16[4,144,128]{2,1,0:T(8,128)(2,1)S(1)}, bf16[4,144,128]{2,1,0:T(8,128)(2,1)S(1)}, u32[]{:S(2)}, u32[]{:S(2)}) collective-permute-start(bf16[4,144,128]{2,1,0:T(8,128)(2,1)S(1)} %get-tuple-element.31), channel_id=1, source_target_pairs={{0,48},{16,0},{32,16},{48,32},{1,49},{17,1},{33,17},{49,33},{2,50}... | collective-permute-start | bytes 442376 | tf_op jit(solution)/shard_map/ppermute | solution.py:280
  63.2 7.0 %collective-permute-done.8.a_ref = bf16[4,144,128]{2,1,0:T(8,128)(2,1)S(1)} collective-permute-done((bf16[4,144,128]{2,1,0:T(8,128)(2,1)S(1)}, bf16[4,144,128]{2,1,0:T(8,128)(2,1)S(1)}, u32[]{:S(2)}, u32[]{:S(2)}) %collective-permute-start.8) | collective-permute-done | bytes 147488 | tf_op jit(solution)/shard_map/ppermute | solution.py:280
  70.2 0.0 collective-permute-done.9.b_ref
  70.2 0.6 collective-permute-done.10.c_ref
  70.8 0.1 shard_map.124
  70.9 0.1 collective-permute-start.11
  71.0 1.7 %collective-permute-start.12 = (bf16[144,128]{1,0:T(8,128)(2,1)S(1)}, bf16[144,128]{1,0:T(8,128)(2,1)S(1)}, u32[]{:S(2)}, u32[]{:S(2)}) collective-permute-start(bf16[144,128]{1,0:T(8,128)(2,1)S(1)} %get-tuple-element.34), channel_id=1, source_target_pairs={{0,128},{64,192},{128,0},{192,64},{1,129},{65,193},{129,1},{193,65... | collective-permute-start | bytes 110600 | tf_op jit(solution)/shard_map/ppermute | solution.py:286
  72.8 1.9 %collective-permute-start.13 = (bf16[144,128]{1,0:T(8,128)(2,1)S(1)}, bf16[144,128]{1,0:T(8,128)(2,1)S(1)}, u32[]{:S(2)}, u32[]{:S(2)}) collective-permute-start(bf16[144,128]{1,0:T(8,128)(2,1)S(1)} %get-tuple-element.35), channel_id=1, source_target_pairs={{0,192},{64,0},{128,64},{192,128},{1,193},{65,1},{129,65},{193,129... | collective-permute-start | bytes 110600 | tf_op jit(solution)/shard_map/ppermute | solution.py:286
  74.6 1.5 %collective-permute-done.11.a_ref = bf16[144,128]{1,0:T(8,128)(2,1)S(1)} collective-permute-done((bf16[144,128]{1,0:T(8,128)(2,1)S(1)}, bf16[144,128]{1,0:T(8,128)(2,1)S(1)}, u32[]{:S(2)}, u32[]{:S(2)}) %collective-permute-start.11) | collective-permute-done | bytes 36896 | tf_op jit(solution)/shard_map/ppermute | solution.py:286
  76.2 0.4 collective-permute-done.12.b_ref
  76.6 0.9 %collective-permute-done.13.c_ref = bf16[144,128]{1,0:T(8,128)(2,1)S(1)} collective-permute-done((bf16[144,128]{1,0:T(8,128)(2,1)S(1)}, bf16[144,128]{1,0:T(8,128)(2,1)S(1)}, u32[]{:S(2)}, u32[]{:S(2)}) %collective-permute-start.13) | collective-permute-done | bytes 36896 | tf_op jit(solution)/shard_map/ppermute | solution.py:286
  77.4 0.0 copy-done.6
  77.4 0.7 shard_map.125
  78.2 0.0 all-to-all-done.1.got_ref
  78.2 0.0 copy-done.5
  78.2 1.9 %shard_map.122 = (f32[256,128]{1,0:T(8,128)}, f32[256,128]{1,0:T(8,128)}) custom-call(bf16[8,272,128]{2,1,0:T(8,128)(2,1)S(1)} %all-to-all-done.1.got_ref, bf16[8,272,128]{2,1,0:T(8,128)(2,1)} %get-tuple-element.21.weight_ref, f32[1,256]{1,0:T(1,128)S(1)} %bitcast.16), custom_call_target="tpu_custom_call" | custom-call | tf_op jit(solution)/shard_map/pallas_call | solution.py:231
  (14 shorter events, 0.1 us)
Async XLA Ops:
  0.6 0.9 %copy-start.1 = (f32[256,128]{1,0:T(8,128)S(1)}, f32[256,128]{1,0:T(8,128)}, u32[]{:S(2)}) copy-start(f32[256,128]{1,0:T(8,128)} %ts_ref.1) | copy-start | bytes 393220
  1.5 0.9 %copy-start.2 = (f32[256,128]{1,0:T(8,128)S(1)}, f32[256,128]{1,0:T(8,128)}, u32[]{:S(2)}) copy-start(f32[256,128]{1,0:T(8,128)} %tr_ref.1) | copy-start | bytes 393220
  2.4 0.8 %copy-start.3 = (f32[128,128]{1,0:T(8,128)S(1)}, f32[128,128]{1,0:T(8,128)}, u32[]{:S(2)}) copy-start(f32[128,128]{1,0:T(8,128)} %bs_ref.1) | copy-start | bytes 196612
  3.3 0.8 %copy-start.4 = (f32[128,128]{1,0:T(8,128)S(1)}, f32[128,128]{1,0:T(8,128)}, u32[]{:S(2)}) copy-start(f32[128,128]{1,0:T(8,128)} %br_ref.1) | copy-start | bytes 196612
  4.1 73.3 %copy-start.6 = (f32[128]{0:T(128)S(1)}, f32[128]{0:T(128)}, u32[]{:S(2)}) copy-start(f32[128]{0:T(128)} %param.14) | copy-start | bytes 1540
  5.1 73.0 %copy-start.5 = (f32[256]{0:T(256)S(1)}, f32[256]{0:T(256)}, u32[]{:S(2)}) copy-start(f32[256]{0:T(256)} %param.11) | copy-start | bytes 3076
  5.1 13.0 %collective-permute-start.2 = (bf16[144,128]{1,0:T(8,128)(2,1)S(1)}, bf16[144,128]{1,0:T(8,128)(2,1)S(1)}, u32[]{:S(2)}, u32[]{:S(2)}) collective-permute-start(bf16[144,128]{1,0:T(8,128)(2,1)S(1)} %get-tuple-element.22.weight_ref), channel_id=1, source_target_pairs={{0,48},{16,0},{32,16},{48,32},{1,49},{17,1},{33,17},{49,33},{2,50}... | collective-permute-start | bytes 110600 | tf_op jit(solution)/shard_map/ppermute | solution.py:266
  7.9 10.3 %collective-permute-start.1 = (bf16[144,128]{1,0:T(8,128)(2,1)S(1)}, bf16[144,128]{1,0:T(8,128)(2,1)S(1)}, u32[]{:S(2)}, u32[]{:S(2)}) collective-permute-start(bf16[144,128]{1,0:T(8,128)(2,1)S(1)} %get-tuple-element.22.weight_ref), channel_id=1, source_target_pairs={{0,32},{16,48},{32,0},{48,16},{1,33},{17,49},{33,1},{49,17},{2,34}... | collective-permute-start | bytes 110600 | tf_op jit(solution)/shard_map/ppermute | solution.py:266
  8.7 9.5 %collective-permute-start = (bf16[144,128]{1,0:T(8,128)(2,1)S(1)}, bf16[144,128]{1,0:T(8,128)(2,1)S(1)}, u32[]{:S(2)}, u32[]{:S(2)}) collective-permute-start(bf16[144,128]{1,0:T(8,128)(2,1)S(1)} %get-tuple-element.22.weight_ref), channel_id=1, source_target_pairs={{0,16},{16,32},{32,48},{48,0},{1,17},{17,33},{33,49},{49,1},{2,18}... | collective-permute-start | bytes 110600 | tf_op jit(solution)/shard_map/ppermute | solution.py:266
  9.6 24.5 %all-to-all-start = ((bf16[8,272,128]{2,1,0:T(8,128)(2,1)}), bf16[8,272,128]{2,1,0:T(8,128)(2,1)S(1)}, u32[]{:S(2)}, u32[]{:S(2)}) async-start(bf16[8,272,128]{2,1,0:T(8,128)(2,1)} %get-tuple-element.21.weight_ref), calls=%async_computation | async-start | bytes 1114112 | tf_op jit(solution)/shard_map/all_to_all | solution.py:265
  18.2 11.7 %collective-permute-start.5 = (bf16[4,144,128]{2,1,0:T(8,128)(2,1)S(1)}, bf16[4,144,128]{2,1,0:T(8,128)(2,1)S(1)}, u32[]{:S(2)}, u32[]{:S(2)}) collective-permute-start(bf16[4,144,128]{2,1,0:T(8,128)(2,1)S(1)} %pad_maximum_fusion), channel_id=1, source_target_pairs={{0,192},{64,0},{128,64},{192,128},{1,193},{65,1},{129,65},{193,129... | collective-permute-start | bytes 442376 | tf_op jit(solution)/shard_map/ppermute | solution.py:267
  21.3 8.6 %collective-permute-start.4 = (bf16[4,144,128]{2,1,0:T(8,128)(2,1)S(1)}, bf16[4,144,128]{2,1,0:T(8,128)(2,1)S(1)}, u32[]{:S(2)}, u32[]{:S(2)}) collective-permute-start(bf16[4,144,128]{2,1,0:T(8,128)(2,1)S(1)} %pad_maximum_fusion), channel_id=1, source_target_pairs={{0,128},{64,192},{128,0},{192,64},{1,129},{65,193},{129,1},{193,65... | collective-permute-start | bytes 442376 | tf_op jit(solution)/shard_map/ppermute | solution.py:267
  21.9 7.9 %collective-permute-start.3 = (bf16[4,144,128]{2,1,0:T(8,128)(2,1)S(1)}, bf16[4,144,128]{2,1,0:T(8,128)(2,1)S(1)}, u32[]{:S(2)}, u32[]{:S(2)}) collective-permute-start(bf16[4,144,128]{2,1,0:T(8,128)(2,1)S(1)} %pad_maximum_fusion), channel_id=1, source_target_pairs={{0,64},{64,128},{128,192},{192,0},{1,65},{65,129},{129,193},{193,1... | collective-permute-start | bytes 442376 | tf_op jit(solution)/shard_map/ppermute | solution.py:267
  30.0 2.1 %collective-permute-start.6 = (bf16[16,144,128]{2,1,0:T(8,128)(2,1)S(1)}, bf16[16,144,128]{2,1,0:T(8,128)(2,1)S(1)}, u32[]{:S(2)}, u32[]{:S(2)}) collective-permute-start(bf16[16,144,128]{2,1,0:T(8,128)(2,1)S(1)} %constant_dynamic-update-slice_fusion.own_ref), channel_id=1, source_target_pairs={{0,8},{8,0},{1,9},{9,1},{2,10},{10,2},{3,11},{11,3},{4,12},{12,4},... | collective-permute-start | bytes 1769480 | tf_op jit(solution)/shard_map/ppermute | solution.py:268
  34.1 3.4 %copy-start = (bf16[1,16,2048,128]{3,2,1,0:T(8,128)(2,1)S(1)}, bf16[1,16,2048,128]{3,2,1,0:T(8,128)(2,1)}, u32[]{:S(2)}) copy-start(bf16[1,16,2048,128]{3,2,1,0:T(8,128)(2,1)} %param.17) | copy-start | bytes 25165828
  37.4 0.7 copy-start.7
  52.5 25.7 %all-to-all-start.1 = ((bf16[8,272,128]{2,1,0:T(8,128)(2,1)}), bf16[8,272,128]{2,1,0:T(8,128)(2,1)S(1)}, u32[]{:S(2)}, u32[]{:S(2)}) async-start(bf16[8,272,128]{2,1,0:T(8,128)(2,1)} %get-tuple-element.23), calls=%async_computation.1 | async-start | bytes 1114112 | tf_op jit(solution)/shard_map/all_to_all | solution.py:273
  57.7 2.0 %collective-permute-start.7 = (bf16[16,144,128]{2,1,0:T(8,128)(2,1)S(1)}, bf16[16,144,128]{2,1,0:T(8,128)(2,1)S(1)}, u32[]{:S(2)}, u32[]{:S(2)}) collective-permute-start(bf16[16,144,128]{2,1,0:T(8,128)(2,1)S(1)} %get-tuple-element.27), channel_id=1, source_target_pairs={{0,8},{8,0},{1,9},{9,1},{2,10},{10,2},{3,11},{11,3},{4,12},{12,4},... | collective-permute-start | bytes 1769480 | tf_op jit(solution)/shard_map/ppermute | solution.py:274
  59.9 10.3 %collective-permute-start.8 = (bf16[4,144,128]{2,1,0:T(8,128)(2,1)S(1)}, bf16[4,144,128]{2,1,0:T(8,128)(2,1)S(1)}, u32[]{:S(2)}, u32[]{:S(2)}) collective-permute-start(bf16[4,144,128]{2,1,0:T(8,128)(2,1)S(1)} %get-tuple-element.29), channel_id=1, source_target_pairs={{0,16},{16,32},{32,48},{48,0},{1,17},{17,33},{33,49},{49,1},{2,18}... | collective-permute-start | bytes 442376 | tf_op jit(solution)/shard_map/ppermute | solution.py:280
  60.0 10.2 %collective-permute-start.9 = (bf16[4,144,128]{2,1,0:T(8,128)(2,1)S(1)}, bf16[4,144,128]{2,1,0:T(8,128)(2,1)S(1)}, u32[]{:S(2)}, u32[]{:S(2)}) collective-permute-start(bf16[4,144,128]{2,1,0:T(8,128)(2,1)S(1)} %get-tuple-element.30), channel_id=1, source_target_pairs={{0,32},{16,48},{32,0},{48,16},{1,33},{17,49},{33,1},{49,17},{2,34}... | collective-permute-start | bytes 442376 | tf_op jit(solution)/shard_map/ppermute | solution.py:280
  61.1 9.8 %collective-permute-start.10 = (bf16[4,144,128]{2,1,0:T(8,128)(2,1)S(1)}, bf16[4,144,128]{2,1,0:T(8,128)(2,1)S(1)}, u32[]{:S(2)}, u32[]{:S(2)}) collective-permute-start(bf16[4,144,128]{2,1,0:T(8,128)(2,1)S(1)} %get-tuple-element.31), channel_id=1, source_target_pairs={{0,48},{16,0},{32,16},{48,32},{1,49},{17,1},{33,17},{49,33},{2,50}... | collective-permute-start | bytes 442376 | tf_op jit(solution)/shard_map/ppermute | solution.py:280
  70.9 5.2 %collective-permute-start.11 = (bf16[144,128]{1,0:T(8,128)(2,1)S(1)}, bf16[144,128]{1,0:T(8,128)(2,1)S(1)}, u32[]{:S(2)}, u32[]{:S(2)}) collective-permute-start(bf16[144,128]{1,0:T(8,128)(2,1)S(1)} %get-tuple-element.33), channel_id=1, source_target_pairs={{0,64},{64,128},{128,192},{192,0},{1,65},{65,129},{129,193},{193,1... | collective-permute-start | bytes 110600 | tf_op jit(solution)/shard_map/ppermute | solution.py:286
  71.0 5.5 %collective-permute-start.12 = (bf16[144,128]{1,0:T(8,128)(2,1)S(1)}, bf16[144,128]{1,0:T(8,128)(2,1)S(1)}, u32[]{:S(2)}, u32[]{:S(2)}) collective-permute-start(bf16[144,128]{1,0:T(8,128)(2,1)S(1)} %get-tuple-element.34), channel_id=1, source_target_pairs={{0,128},{64,192},{128,0},{192,64},{1,129},{65,193},{129,1},{193,65... | collective-permute-start | bytes 110600 | tf_op jit(solution)/shard_map/ppermute | solution.py:286
  72.8 4.7 %collective-permute-start.13 = (bf16[144,128]{1,0:T(8,128)(2,1)S(1)}, bf16[144,128]{1,0:T(8,128)(2,1)S(1)}, u32[]{:S(2)}, u32[]{:S(2)}) collective-permute-start(bf16[144,128]{1,0:T(8,128)(2,1)S(1)} %get-tuple-element.35), channel_id=1, source_target_pairs={{0,192},{64,0},{128,64},{192,128},{1,193},{65,1},{129,65},{193,129... | collective-permute-start | bytes 110600 | tf_op jit(solution)/shard_map/ppermute | solution.py:286

commit v2 on v1

v2 whole, which is shorter than its diff:
```python
import jax
import jax.numpy as jnp
from jax import lax
from jax.experimental import pallas as pl
from jax.experimental.pallas import tpu as pltpu
from jax.sharding import Mesh, PartitionSpec as P

F32 = jnp.float32
BF16 = jnp.bfloat16
VMEM = pl.BlockSpec(memory_space=pltpu.VMEM)
HBM = pl.BlockSpec(memory_space=pltpu.HBM)
EXTRA = 16
CHUNK = 1024
GROUP = 4


def params(mib):
    return pltpu.CompilerParams(vmem_limit_bytes=mib * 1024 * 1024)


def digamma_series(value):
    shifted = value
    correction = jnp.zeros_like(value)
    for offset in range(6):
        correction = correction + 1.0 / shifted
        shifted = shifted + 1.0
    inverse = 1.0 / shifted
    square = inverse * inverse
    series = (
        jnp.log(shifted)
        - 0.5 * inverse
        - square * (1.0 / 12.0 - square * (1.0 / 120.0 - square * (1.0 / 252.0)))
    )
    return series - correction


def split_rows(total):
    high = total.astype(BF16).astype(F32)
    middle = (total - high).astype(BF16).astype(F32)
    low = total - high - middle
    row = lax.broadcasted_iota(jnp.int32, (EXTRA, total.shape[1]), 0)
    block = jnp.where(row == 0, high, jnp.where(row == 1, middle, jnp.where(row == 2, low, 0.0)))
    return block.astype(BF16)


def row_total(block):
    return jnp.sum(block.astype(F32), axis=0, keepdims=True)


def weights_kernel(ts_hbm, tr_hbm, bs_hbm, br_hbm, cell_ref, gene_ref, ts_s, tr_s, bs_s, br_s, sems):
    pairs = ((bs_hbm, bs_s), (br_hbm, br_s), (ts_hbm, ts_s), (tr_hbm, tr_s))
    moves = [pltpu.make_async_copy(*pair, sems.at[index]) for index, pair in enumerate(pairs)]
    for move in moves:
        move.start()
    moves[0].wait()
    moves[1].wait()
    shape, rate = bs_s[...], br_s[...]
    genes = shape.shape[0]
    gene_ref[:genes] = jnp.exp(digamma_series(shape) - jnp.log(rate)).astype(BF16)
    gene_ref[genes:] = split_rows(jnp.sum(shape / rate, axis=0, keepdims=True))
    moves[2].wait()
    moves[3].wait()
    shape, rate = ts_s[...], tr_s[...]
    copies, cells = cell_ref.shape[0], shape.shape[0]
    weight = jnp.exp(digamma_series(shape) - jnp.log(rate)).astype(BF16)
    extra = split_rows(jnp.sum(shape / rate, axis=0, keepdims=True))
    for copy in range(copies):
        cell_ref[copy, :cells] = weight
        cell_ref[copy, cells:] = extra


def weights_call(theta_shape, theta_rate, beta_shape, beta_rate):
    cells, width = theta_shape.shape
    genes = beta_shape.shape[0]
    return pl.pallas_call(
        weights_kernel,
        in_specs=[HBM] * 4,
        out_specs=[VMEM] * 2,
        out_shape=[
            jax.ShapeDtypeStruct((8, cells + EXTRA, width), BF16),
            jax.ShapeDtypeStruct((genes + EXTRA, width), BF16),
        ],
        scratch_shapes=[pltpu.VMEM((cells, width), F32)] * 2
        + [pltpu.VMEM((genes, width), F32)] * 2
        + [pltpu.SemaphoreType.DMA((4,))],
        compiler_params=params(16),
    )(theta_shape, theta_rate, beta_shape, beta_rate)


def main_kernel(
    ids_ref, live_ref, cell_ref, own_ref, oth_ref, counts_ref,
    cell_out, keep_out, send_out,
    ids_s, live_s, counts_s, rows_s, cols_s, acc_s, gene_s, sems, id_sem, live_sem,
):
    parts, padded, width = cell_ref.shape
    part = padded - EXTRA
    block = own_ref.shape[1] - EXTRA
    sides = own_ref.shape[0]
    cells = parts * part
    groups = counts_ref.shape[0] // GROUP
    my_y, my_x, my_core = lax.axis_index("y"), lax.axis_index("x"), lax.axis_index("core")

    def fetch(group):
        here = pl.ds(group * GROUP, GROUP)
        return pltpu.make_async_copy(counts_ref.at[here], counts_s.at[here], sems.at[group])

    live_copy = pltpu.make_async_copy(live_ref, live_s, live_sem)
    ids_copy = pltpu.make_async_copy(ids_ref, ids_s, id_sem)
    live_copy.start()
    ids_copy.start()
    fetch(0).start()
    for index in range(parts):
        rows = cell_ref[index, :part]
        rows_s[pl.ds(index * part, part), :] = rows
        cols_s[:, pl.ds(index * part, part)] = rows.T
    gene_s[...] = jnp.zeros_like(gene_s)
    live_copy.wait()
    ids_copy.wait()
    live = live_s[0, 0]
    for group in range(1, groups):
        @pl.when(GROUP * group < live)
        def _():
            fetch(group).start()

    def place(slot):
        index = ids_s[0, 0, slot]
        core, x, y = index % 2, (index // 2) % 4, index // 8
        from_x, from_y = (my_x - x + 4) % 4, (my_y - y + 4) % 4
        spot = jnp.where(core == 0, from_y * 4 + from_x, from_x * 4 + from_y)
        return index, core == my_core, spot

    def block_of(slot):
        _, mine, spot = place(slot)
        return jnp.where(mine, own_ref[spot, :block], oth_ref[spot, :block])

    for group in range(groups):
        @pl.when(GROUP * group < live)
        def _():
            slots = [GROUP * group + index for index in range(GROUP)]
            alive = [slot < live for slot in slots]
            pair = jnp.concatenate([block_of(slot) for slot in slots], axis=0)
            fetch(group).wait()
            total = jnp.zeros((width, GROUP * block), F32)
            for start in range(0, cells, CHUNK):
                here = pl.ds(start, CHUNK)
                rate = lax.dot_general(
                    rows_s[here, :], pair, (((1,), (1,)), ((), ())), preferred_element_type=F32
                )
                ratios = []
                for index in range(GROUP):
                    columns = slice(index * block, (index + 1) * block)
                    ratio = counts_s[slots[index], here, :].astype(F32) / rate[:, columns]
                    if slots[index] > 1:
                        ratio = jnp.where(alive[index], ratio, 0.0)
                    ratios.append(ratio.astype(BF16))
                ratio = jnp.concatenate(ratios, axis=1)
                term = jnp.dot(ratio, pair, preferred_element_type=F32)
                if group == 0:
                    acc_s[here, :] = term
                else:
                    acc_s[here, :] += term
                total += jnp.dot(cols_s[:, here], ratio, preferred_element_type=F32)
            total = total.T
            for k in range(GROUP):
                @pl.when(alive[k])
                def _():
                    index, mine, _ = place(slots[k])
                    gene_s[jnp.where(mine, 0, 1), index // 2] = total[k * block : (k + 1) * block]

    theta = row_total(cell_ref[:, part:].reshape(parts * EXTRA, width))
    beta = row_total(own_ref[:, block:].reshape(sides * EXTRA, width))
    beta += row_total(oth_ref[:, block:].reshape(sides * EXTRA, width))
    theta, beta = split_rows(theta), split_rows(beta)
    for index in range(parts):
        cell_out[index, :part] = acc_s[pl.ds(index * part, part), :].astype(BF16)
        cell_out[index, part:] = beta
    for index in range(sides):
        keep_out[index, :block] = gene_s[0, index]
        keep_out[index, block:] = theta.astype(F32)
        send_out[index, :block] = gene_s[1, index].astype(BF16)
        send_out[index, block:] = theta


def main_call(ids, live, cell_rows, own, other, counts):
    slots, cells, block = counts.shape
    parts, padded, width = cell_rows.shape
    sides, tall, _ = own.shape
    return pl.pallas_call(
        main_kernel,
        in_specs=[HBM, HBM, VMEM, VMEM, VMEM, HBM],
        out_specs=[VMEM, VMEM, VMEM],
        scratch_shapes=[
            pltpu.SMEM(ids.shape, jnp.int32),
            pltpu.SMEM(live.shape, jnp.int32),
            pltpu.VMEM((slots, cells, block), BF16),
            pltpu.VMEM((cells, width), BF16),
            pltpu.VMEM((width, cells), BF16),
            pltpu.VMEM((cells, width), F32),
            pltpu.VMEM((2, sides, block, width), F32),
            pltpu.SemaphoreType.DMA((slots // GROUP,)),
            pltpu.SemaphoreType.DMA,
            pltpu.SemaphoreType.DMA,
        ],
        out_shape=[
            jax.ShapeDtypeStruct((parts, padded, width), BF16),
            jax.ShapeDtypeStruct((sides, tall, width), F32),
            jax.ShapeDtypeStruct((sides, tall, width), BF16),
        ],
        compiler_params=params(48),
    )(ids, live, cell_rows, own, other, counts)


def first_and_second():
    my_y, my_x, core = lax.axis_index("y"), lax.axis_index("x"), lax.axis_index("core")
    return core, jnp.where(core == 0, my_x, my_y), jnp.where(core == 0, my_y, my_x)


def core_sum_kernel(keep_ref, got_ref, mine_ref, *send_refs):
    core, first, _ = first_and_second()
    for row in range(4):
        for step in range(4):
            along = (first + step) % 4
            spot = jnp.where(core == 0, row * 4 + along, along * 4 + row)
            value = keep_ref[spot] + got_ref[spot].astype(F32)
            if step == 0:
                mine_ref[row] = value
            else:
                send_refs[step - 1][row] = respread(value)


def respread(value):
    rows = value.shape[0] - EXTRA
    return jnp.concatenate([value[:rows].astype(BF16), split_rows(row_total(value[rows:]))], axis=0)


def first_sum_kernel(keep_ref, a_ref, b_ref, c_ref, mine_ref, *send_refs):
    _, _, second = first_and_second()
    for step in range(4):
        spot = (second + step) % 4
        value = keep_ref[spot] + a_ref[spot].astype(F32)
        value += b_ref[spot].astype(F32) + c_ref[spot].astype(F32)
        if step == 0:
            mine_ref[...] = value
        else:
            send_refs[step - 1][...] = respread(value)


def finish(weight, stat, activity, total, shape_ref, rate_ref):
    rows, width = stat.shape
    shape_ref[...] = jnp.log(0.3 + weight.astype(F32) * stat)
    for start in range(0, rows, 128):
        here = pl.ds(start, 128)
        column = jnp.broadcast_to(activity[:, start : start + 128], (width, 128)).T
        rate_ref[here, :] = jnp.log(column + total)


def gene_finish_kernel(keep_ref, a_ref, b_ref, c_ref, weight_ref, act_ref, shape_ref, rate_ref):
    value = keep_ref[...] + a_ref[...].astype(F32)
    value += b_ref[...].astype(F32) + c_ref[...].astype(F32)
    rows = value.shape[0] - EXTRA
    total = row_total(value[rows:])
    finish(weight_ref[:rows], value[:rows], act_ref[...], total, shape_ref, rate_ref)


def cell_finish_kernel(got_ref, weight_ref, act_ref, shape_ref, rate_ref):
    parts = got_ref.shape[0]
    rows = got_ref.shape[1] - EXTRA
    value = got_ref[0].astype(F32)
    for index in range(1, parts):
        value += got_ref[index].astype(F32)
    total = row_total(value[rows:])
    finish(weight_ref[0, :rows], value[:rows], act_ref[...], total, shape_ref, rate_ref)


def simple_call(kernel, out_shape, *args, mib=16):
    return pl.pallas_call(
        kernel,
        in_specs=[VMEM] * len(args),
        out_specs=[VMEM] * len(out_shape),
        out_shape=out_shape,
        compiler_params=params(mib),
    )(*args)


def shift(stage, step, value):
    pairs = []
    for y in range(4):
        for x in range(4):
            for core in range(2):
                if core == stage:
                    to_y, to_x = y, (x + step) % 4
                else:
                    to_y, to_x = (y + step) % 4, x
                pairs.append(((y * 4 + x) * 2 + core, (to_y * 4 + to_x) * 2 + core))
    return lax.ppermute(value, ("y", "x", "core"), pairs)


def swap_cores(value):
    return lax.ppermute(value, "core", [(0, 1), (1, 0)])


def on_device(
    theta_shape,
    theta_rate,
    cell_activity,
    beta_shape,
    beta_rate,
    gene_activity,
    block_ids,
    live_blocks,
    counts,
):
    cells, width = theta_shape.shape
    genes = beta_shape.shape[0]
    tall = genes + EXTRA
    struct = jax.ShapeDtypeStruct
    steps = (1, 2, 3)
    cell_pay, gene_pay = weights_call(theta_shape, theta_rate, beta_shape, beta_rate)
    cell_rows = lax.all_to_all(cell_pay, "z", 0, 0)
    line = jnp.stack([gene_pay] + [shift(0, step, gene_pay) for step in steps])
    own = jnp.concatenate([line] + [shift(1, step, line) for step in steps])
    other = swap_cores(own)

    cell_part, keep, send = main_call(block_ids, live_blocks, cell_rows, own, other, counts[0])
    cell_got = lax.all_to_all(cell_part, "z", 0, 0)
    keep, *sends = simple_call(
        core_sum_kernel,
        [struct((4, tall, width), F32)] + [struct((4, tall, width), BF16)] * 3,
        keep, swap_cores(send),
    )
    gots = [shift(0, step, sends[step - 1]) for step in steps]
    keep, *sends = simple_call(
        first_sum_kernel,
        [struct((tall, width), F32)] + [struct((tall, width), BF16)] * 3,
        keep, *gots,
    )
    gots = [shift(1, step, sends[step - 1]) for step in steps]
    log_theta = simple_call(
        cell_finish_kernel, [struct((cells, width), F32)] * 2,
        cell_got, cell_pay, cell_activity.reshape(1, cells),
    )
    gots, log_theta = lax.optimization_barrier((gots, log_theta))
    log_beta = simple_call(
        gene_finish_kernel, [struct((genes, width), F32)] * 2,
        keep, *gots, gene_pay, gene_activity.reshape(1, genes),
    )
    return (*log_theta, *log_beta)


def solution(mesh):
    fine = Mesh(mesh.devices.reshape(4, 4, 2, 8), ("y", "x", "core", "z"))
    cells = ("y", "x", "core")
    every = cells + ("z",)
    in_specs = (
        P(every, None),
        P(every, None),
        P(every),
        P(every, None),
        P(every, None),
        P(every),
        P("z", cells, None),
        P("z", cells),
        P("z", None, cells, None),
    )
    out_specs = (P(every, None),) * 4
    return jax.shard_map(
        on_device, mesh=fine, in_specs=in_specs, out_specs=out_specs, check_vma=False
    )
```

time: 81.4 us -> 70.7 us (0.87)
  the two profiles are of different devices: /device:TPU:32 before, /device:TPU:6 now
where the time goes in v2:
time: 70.7 us; the launch traced here: 70.2 us
  starting transfers between devices  32.2 us (46%)
  waiting for transfers between devices  21.6 us (31%)
  Pallas kernels  10.7 us (15%)
  local copies, waits for them, and re-layouts  4.24 us (6%)
  between operations  1.42 us (2%)
    ppermute x12, starting transfers between devices, shift(): return lax.ppermute(value, ('y', 'x', 'core'), pairs)  18.1 us
    ppermute x12, waiting for transfers between devices, shift(): return lax.ppermute(value, ('y', 'x', 'core'), pairs)  13.9 us
    all_to_all x1, starting transfers between devices, on_device(): cell_rows = lax.all_to_all(cell_pay, 'z', 0, 0)  8.47 us
    pallas_call x1, Pallas kernels, main_call(): pl.pallas_call(main_kernel, in_specs=[HBM, HBM, VMEM, VMEM, VMEM, HBM], o...  6.21 us
    all_to_all x1, starting transfers between devices, on_device(): cell_got = lax.all_to_all(cell_part, 'z', 0, 0)  5.52 us
    all_to_all x1, waiting for transfers between devices, on_device(): cell_rows = lax.all_to_all(cell_pay, 'z', 0, 0)  4.34 us
    unnamed x20, local copies, waits for them, and re-layouts  4.22 us
    ppermute x2, waiting for transfers between devices, swap_cores(): return lax.ppermute(value, 'core', [(0, 1), (1, 0)])  3.34 us
  transfers between devices with their start and end apart: 16, of which 8 were waited for; matrix products, arithmetic and copies ran while one was open for 0% of the time, Pallas kernels for 3%

profile of v2, /device:TPU:6, one launch (start us, length us, event | category | flops | bytes accessed | tf_op | source)
XLA Modules:
  0.0 70.2 jit_solution(3730613823169573512)
XLA Ops:
  0.6 0.0 copy-start
  0.6 0.9 %copy-done = f32[256,128]{1,0:T(8,128)S(1)} copy-done((f32[256,128]{1,0:T(8,128)S(1)}, f32[256,128]{1,0:T(8,128)}, u32[]{:S(2)}) %copy-start) | copy-done | bytes 131096
  1.5 0.0 copy-start.1
  1.5 0.9 %copy-done.1 = f32[256,128]{1,0:T(8,128)S(1)} copy-done((f32[256,128]{1,0:T(8,128)S(1)}, f32[256,128]{1,0:T(8,128)}, u32[]{:S(2)}) %copy-start.1) | copy-done | bytes 131096
  2.4 0.0 copy-start.2
  2.4 0.8 %copy-done.2 = f32[128,128]{1,0:T(8,128)S(1)} copy-done((f32[128,128]{1,0:T(8,128)S(1)}, f32[128,128]{1,0:T(8,128)}, u32[]{:S(2)}) %copy-start.2) | copy-done | bytes 65560
  3.3 0.8 %copy-done.3 = f32[128,128]{1,0:T(8,128)S(1)} copy-done((f32[128,128]{1,0:T(8,128)S(1)}, f32[128,128]{1,0:T(8,128)}, u32[]{:S(2)}) %copy-start.3) | copy-done | bytes 65560
  4.1 1.7 %shard_map.120 = (bf16[8,272,128]{2,1,0:T(8,128)(2,1)}, bf16[144,128]{1,0:T(8,128)(2,1)S(1)}) custom-call(f32[256,128]{1,0:T(8,128)S(1)} %copy-done, f32[256,128]{1,0:T(8,128)S(1)} %copy-done.1, f32[128,128]{1,0:T(8,128)S(1)} %copy-done.2, f32[128,128]{1,0:T(8,128)S(1)} %copy-done.3), custom_call_target="tpu_custom_call" | custom-call | tf_op jit(solution)/shard_map/pallas_call | solution.py:75
  5.8 0.9 %collective-permute-start.2 = (bf16[144,128]{1,0:T(8,128)(2,1)S(1)}, bf16[144,128]{1,0:T(8,128)(2,1)S(1)}, u32[]{:S(2)}, u32[]{:S(2)}) collective-permute-start(bf16[144,128]{1,0:T(8,128)(2,1)S(1)} %get-tuple-element.27.weight_ref), channel_id=1, source_target_pairs={{0,48},{8,200},{16,0},{24,216},{32,16},{40,232},{48,32},{56,248},{... | collective-permute-start | bytes 110600 | tf_op jit(solution)/shard_map/ppermute | solution.py:295
  6.7 2.8 %collective-permute-start.1 = (bf16[144,128]{1,0:T(8,128)(2,1)S(1)}, bf16[144,128]{1,0:T(8,128)(2,1)S(1)}, u32[]{:S(2)}, u32[]{:S(2)}) collective-permute-start(bf16[144,128]{1,0:T(8,128)(2,1)S(1)} %get-tuple-element.27.weight_ref), channel_id=1, source_target_pairs={{0,32},{8,136},{16,48},{24,152},{32,0},{40,168},{48,16},{56,184},{... | collective-permute-start | bytes 110600 | tf_op jit(solution)/shard_map/ppermute | solution.py:295
  9.6 0.4 collective-permute-start
  9.9 8.5 %all-to-all-start = ((bf16[8,272,128]{2,1,0:T(8,128)(2,1)}), bf16[8,272,128]{2,1,0:T(8,128)(2,1)S(1)}, u32[]{:S(2)}, u32[]{:S(2)}) async-start(bf16[8,272,128]{2,1,0:T(8,128)(2,1)} %get-tuple-element.26.weight_ref), calls=%async_computation | async-start | bytes 1114112 | tf_op jit(solution)/shard_map/all_to_all | solution.py:319
  18.4 0.0 collective-permute-done.2
  18.4 0.0 collective-permute-done.1
  18.4 0.0 collective-permute-done
  18.5 3.1 %collective-permute-start.5 = (bf16[4,144,128]{2,1,0:T(8,128)(2,1)S(1)}, bf16[4,144,128]{2,1,0:T(8,128)(2,1)S(1)}, u32[]{:S(2)}, u32[]{:S(2)}) collective-permute-start(bf16[4,144,128]{2,1,0:T(8,128)(2,1)S(1)} %pad_maximum_fusion), channel_id=1, source_target_pairs={{0,192},{8,56},{16,208},{24,8},{32,224},{40,24},{48,240},{56,40},{... | collective-permute-start | bytes 442376 | tf_op jit(solution)/shard_map/ppermute | solution.py:295
  21.6 0.6 collective-permute-start.4
  22.2 1.0 %collective-permute-start.3 = (bf16[4,144,128]{2,1,0:T(8,128)(2,1)S(1)}, bf16[4,144,128]{2,1,0:T(8,128)(2,1)S(1)}, u32[]{:S(2)}, u32[]{:S(2)}) collective-permute-start(bf16[4,144,128]{2,1,0:T(8,128)(2,1)S(1)} %pad_maximum_fusion), channel_id=1, source_target_pairs={{0,64},{8,24},{16,80},{24,40},{32,96},{40,56},{48,112},{56,8},{64,... | collective-permute-start | bytes 442376 | tf_op jit(solution)/shard_map/ppermute | solution.py:295
  23.2 6.6 %collective-permute-done.3 = bf16[4,144,128]{2,1,0:T(8,128)(2,1)S(1)} collective-permute-done((bf16[4,144,128]{2,1,0:T(8,128)(2,1)S(1)}, bf16[4,144,128]{2,1,0:T(8,128)(2,1)S(1)}, u32[]{:S(2)}, u32[]{:S(2)}) %collective-permute-start.3) | collective-permute-done | bytes 147488 | tf_op jit(solution)/shard_map/ppermute | solution.py:295
  29.8 0.0 collective-permute-done.4
  29.8 0.0 collective-permute-done.5
  29.9 0.1 collective-permute-start.6
  30.6 1.3 %collective-permute-done.6.oth_ref = bf16[16,144,128]{2,1,0:T(8,128)(2,1)S(1)} collective-permute-done((bf16[16,144,128]{2,1,0:T(8,128)(2,1)S(1)}, bf16[16,144,128]{2,1,0:T(8,128)(2,1)S(1)}, u32[]{:S(2)}, u32[]{:S(2)}) %collective-permute-start.6) | collective-permute-done | bytes 589856 | tf_op jit(solution)/shard_map/ppermute | solution.py:299
  32.0 4.3 %all-to-all-done.cell_ref = bf16[8,272,128]{2,1,0:T(8,128)(2,1)S(1)} async-done(((bf16[8,272,128]{2,1,0:T(8,128)(2,1)}), bf16[8,272,128]{2,1,0:T(8,128)(2,1)S(1)}, u32[]{:S(2)}, u32[]{:S(2)}) %all-to-all-start) | async-done | bytes 557088 | tf_op jit(solution)/shard_map/all_to_all | solution.py:319
  36.3 0.7 copy-done.6
  37.0 6.2 %shard_map.121 = (bf16[8,272,128]{2,1,0:T(8,128)(2,1)}, f32[16,144,128]{2,1,0:T(8,128)S(1)}, bf16[16,144,128]{2,1,0:T(8,128)(2,1)S(1)}) custom-call(s32[1,1,16]{2,1,0:T(1,128)S(1)} %copy-done.6, s32[1,1]{1,0:T(1,128)S(6)} %copy.19.live_ref, bf16[8,272,128]{2,1,0:T(8,128)(2,1)S(1)} %all-to-all-done.cell_ref, ...), custom_call_target="tpu_custom_call" | custom-call | tf_op jit(solution)/shard_map/pallas_call | solution.py:188
  43.2 5.5 %all-to-all-start.1 = ((bf16[8,272,128]{2,1,0:T(8,128)(2,1)}), bf16[8,272,128]{2,1,0:T(8,128)(2,1)S(1)}, u32[]{:S(2)}, u32[]{:S(2)}) async-start(bf16[8,272,128]{2,1,0:T(8,128)(2,1)} %get-tuple-element.37), calls=%async_computation.1 | async-start | bytes 1114112 | tf_op jit(solution)/shard_map/all_to_all | solution.py:325
  48.7 0.0 collective-permute-start.7
  48.7 2.0 %collective-permute-done.7.got_ref = bf16[16,144,128]{2,1,0:T(8,128)(2,1)S(1)} collective-permute-done((bf16[16,144,128]{2,1,0:T(8,128)(2,1)S(1)}, bf16[16,144,128]{2,1,0:T(8,128)(2,1)S(1)}, u32[]{:S(2)}, u32[]{:S(2)}) %collective-permute-start.7) | collective-permute-done | bytes 589856 | tf_op jit(solution)/shard_map/ppermute | solution.py:299
  50.7 0.2 shard_map.122
  50.9 1.9 %collective-permute-start.8 = (bf16[4,144,128]{2,1,0:T(8,128)(2,1)S(1)}, bf16[4,144,128]{2,1,0:T(8,128)(2,1)S(1)}, u32[]{:S(2)}, u32[]{:S(2)}) collective-permute-start(bf16[4,144,128]{2,1,0:T(8,128)(2,1)S(1)} %get-tuple-element.31), channel_id=1, source_target_pairs={{0,16},{8,72},{16,32},{24,88},{32,48},{40,104},{48,0},{56,120},{64... | collective-permute-start | bytes 442376 | tf_op jit(solution)/shard_map/ppermute | solution.py:295
  52.7 0.4 collective-permute-start.9
  53.2 1.3 %collective-permute-start.10 = (bf16[4,144,128]{2,1,0:T(8,128)(2,1)S(1)}, bf16[4,144,128]{2,1,0:T(8,128)(2,1)S(1)}, u32[]{:S(2)}, u32[]{:S(2)}) collective-permute-start(bf16[4,144,128]{2,1,0:T(8,128)(2,1)S(1)} %get-tuple-element.33), channel_id=1, source_target_pairs={{0,48},{8,200},{16,0},{24,216},{32,16},{40,232},{48,32},{56,248},{... | collective-permute-start | bytes 442376 | tf_op jit(solution)/shard_map/ppermute | solution.py:295
  54.5 2.5 %collective-permute-done.8.a_ref = bf16[4,144,128]{2,1,0:T(8,128)(2,1)S(1)} collective-permute-done((bf16[4,144,128]{2,1,0:T(8,128)(2,1)S(1)}, bf16[4,144,128]{2,1,0:T(8,128)(2,1)S(1)}, u32[]{:S(2)}, u32[]{:S(2)}) %collective-permute-start.8) | collective-permute-done | bytes 147488 | tf_op jit(solution)/shard_map/ppermute | solution.py:295
  57.0 2.5 %collective-permute-done.9.b_ref = bf16[4,144,128]{2,1,0:T(8,128)(2,1)S(1)} collective-permute-done((bf16[4,144,128]{2,1,0:T(8,128)(2,1)S(1)}, bf16[4,144,128]{2,1,0:T(8,128)(2,1)S(1)}, u32[]{:S(2)}, u32[]{:S(2)}) %collective-permute-start.9) | collective-permute-done | bytes 147488 | tf_op jit(solution)/shard_map/ppermute | solution.py:295
  59.5 1.5 %collective-permute-done.10.c_ref = bf16[4,144,128]{2,1,0:T(8,128)(2,1)S(1)} collective-permute-done((bf16[4,144,128]{2,1,0:T(8,128)(2,1)S(1)}, bf16[4,144,128]{2,1,0:T(8,128)(2,1)S(1)}, u32[]{:S(2)}, u32[]{:S(2)}) %collective-permute-start.10) | collective-permute-done | bytes 147488 | tf_op jit(solution)/shard_map/ppermute | solution.py:295
  61.0 0.1 shard_map.123
  61.1 2.9 %collective-permute-start.11 = (bf16[144,128]{1,0:T(8,128)(2,1)S(1)}, bf16[144,128]{1,0:T(8,128)(2,1)S(1)}, u32[]{:S(2)}, u32[]{:S(2)}) collective-permute-start(bf16[144,128]{1,0:T(8,128)(2,1)S(1)} %get-tuple-element.34), channel_id=1, source_target_pairs={{0,64},{8,24},{16,80},{24,40},{32,96},{40,56},{48,112},{56,8},{64,... | collective-permute-start | bytes 110600 | tf_op jit(solution)/shard_map/ppermute | solution.py:295
  64.0 0.0 collective-permute-start.12
  64.0 2.8 %collective-permute-start.13 = (bf16[144,128]{1,0:T(8,128)(2,1)S(1)}, bf16[144,128]{1,0:T(8,128)(2,1)S(1)}, u32[]{:S(2)}, u32[]{:S(2)}) collective-permute-start(bf16[144,128]{1,0:T(8,128)(2,1)S(1)} %get-tuple-element.36), channel_id=1, source_target_pairs={{0,192},{8,56},{16,208},{24,8},{32,224},{40,24},{48,240},{56,40},{... | collective-permute-start | bytes 110600 | tf_op jit(solution)/shard_map/ppermute | solution.py:295
  66.8 0.0 all-to-all-done.1.got_ref
  66.8 0.0 copy-done.4
  66.8 1.9 %shard_map.124 = (f32[256,128]{1,0:T(8,128)}, f32[256,128]{1,0:T(8,128)}) custom-call(bf16[8,272,128]{2,1,0:T(8,128)(2,1)S(1)} %all-to-all-done.1.got_ref, bf16[8,272,128]{2,1,0:T(8,128)(2,1)} %get-tuple-element.26.weight_ref, f32[1,256]{1,0:T(1,128)S(1)} %bitcast.12), custom_call_target="tpu_custom_call" | custom-call | tf_op jit(solution)/shard_map/pallas_call | solution.py:276
  68.6 0.0 collective-permute-done.11.a_ref
  68.6 0.8 %collective-permute-done.12.b_ref = bf16[144,128]{1,0:T(8,128)(2,1)S(1)} collective-permute-done((bf16[144,128]{1,0:T(8,128)(2,1)S(1)}, bf16[144,128]{1,0:T(8,128)(2,1)S(1)}, u32[]{:S(2)}, u32[]{:S(2)}) %collective-permute-start.12) | collective-permute-done | bytes 36896 | tf_op jit(solution)/shard_map/ppermute | solution.py:295
  69.4 0.0 collective-permute-done.13.c_ref
  69.4 0.0 copy-done.5
  69.4 0.7 %shard_map.125 = (f32[128,128]{1,0:T(8,128)}, f32[128,128]{1,0:T(8,128)}) custom-call(f32[144,128]{1,0:T(8,128)S(1)} %get-tuple-element.42.keep_ref, bf16[144,128]{1,0:T(8,128)(2,1)S(1)} %collective-permute-done.11.a_ref, bf16[144,128]{1,0:T(8,128)(2,1)S(1)} %collective-permute-done.12.b_ref, bf16[144,128]{1,0:T(8,128)(2,1)S(1)} %collective-permute-done.13.c_ref, ...), custom_call_target="tpu_custom_call" | custom-call | tf_op jit(solution)/shard_map/pallas_call | solution.py:276
  (12 shorter events, 0.1 us)
Async XLA Ops:
  0.6 0.9 %copy-start = (f32[256,128]{1,0:T(8,128)S(1)}, f32[256,128]{1,0:T(8,128)}, u32[]{:S(2)}) copy-start(f32[256,128]{1,0:T(8,128)} %ts_hbm.1) | copy-start | bytes 393220
  1.5 0.9 %copy-start.1 = (f32[256,128]{1,0:T(8,128)S(1)}, f32[256,128]{1,0:T(8,128)}, u32[]{:S(2)}) copy-start(f32[256,128]{1,0:T(8,128)} %tr_hbm.1) | copy-start | bytes 393220
  2.4 0.8 %copy-start.2 = (f32[128,128]{1,0:T(8,128)S(1)}, f32[128,128]{1,0:T(8,128)}, u32[]{:S(2)}) copy-start(f32[128,128]{1,0:T(8,128)} %bs_hbm.1) | copy-start | bytes 196612
  3.3 0.8 %copy-start.3 = (f32[128,128]{1,0:T(8,128)S(1)}, f32[128,128]{1,0:T(8,128)}, u32[]{:S(2)}) copy-start(f32[128,128]{1,0:T(8,128)} %br_hbm.1) | copy-start | bytes 196612
  4.1 62.6 %copy-start.4 = (f32[256]{0:T(256)S(1)}, f32[256]{0:T(256)}, u32[]{:S(2)}) copy-start(f32[256]{0:T(256)} %param.11) | copy-start | bytes 3076
  5.8 12.6 %collective-permute-start.2 = (bf16[144,128]{1,0:T(8,128)(2,1)S(1)}, bf16[144,128]{1,0:T(8,128)(2,1)S(1)}, u32[]{:S(2)}, u32[]{:S(2)}) collective-permute-start(bf16[144,128]{1,0:T(8,128)(2,1)S(1)} %get-tuple-element.27.weight_ref), channel_id=1, source_target_pairs={{0,48},{8,200},{16,0},{24,216},{32,16},{40,232},{48,32},{56,248},{... | collective-permute-start | bytes 110600 | tf_op jit(solution)/shard_map/ppermute | solution.py:295
  6.7 11.7 %collective-permute-start.1 = (bf16[144,128]{1,0:T(8,128)(2,1)S(1)}, bf16[144,128]{1,0:T(8,128)(2,1)S(1)}, u32[]{:S(2)}, u32[]{:S(2)}) collective-permute-start(bf16[144,128]{1,0:T(8,128)(2,1)S(1)} %get-tuple-element.27.weight_ref), channel_id=1, source_target_pairs={{0,32},{8,136},{16,48},{24,152},{32,0},{40,168},{48,16},{56,184},{... | collective-permute-start | bytes 110600 | tf_op jit(solution)/shard_map/ppermute | solution.py:295
  9.6 8.9 %collective-permute-start = (bf16[144,128]{1,0:T(8,128)(2,1)S(1)}, bf16[144,128]{1,0:T(8,128)(2,1)S(1)}, u32[]{:S(2)}, u32[]{:S(2)}) collective-permute-start(bf16[144,128]{1,0:T(8,128)(2,1)S(1)} %get-tuple-element.27.weight_ref), channel_id=1, source_target_pairs={{0,16},{8,72},{16,32},{24,88},{32,48},{40,104},{48,0},{56,120},{64... | collective-permute-start | bytes 110600 | tf_op jit(solution)/shard_map/ppermute | solution.py:295
  9.9 26.4 %all-to-all-start = ((bf16[8,272,128]{2,1,0:T(8,128)(2,1)}), bf16[8,272,128]{2,1,0:T(8,128)(2,1)S(1)}, u32[]{:S(2)}, u32[]{:S(2)}) async-start(bf16[8,272,128]{2,1,0:T(8,128)(2,1)} %get-tuple-element.26.weight_ref), calls=%async_computation | async-start | bytes 1114112 | tf_op jit(solution)/shard_map/all_to_all | solution.py:319
  18.4 51.1 %copy-start.5 = (f32[128]{0:T(128)S(1)}, f32[128]{0:T(128)}, u32[]{:S(2)}) copy-start(f32[128]{0:T(128)} %param.14) | copy-start | bytes 1540
  18.5 11.4 %collective-permute-start.5 = (bf16[4,144,128]{2,1,0:T(8,128)(2,1)S(1)}, bf16[4,144,128]{2,1,0:T(8,128)(2,1)S(1)}, u32[]{:S(2)}, u32[]{:S(2)}) collective-permute-start(bf16[4,144,128]{2,1,0:T(8,128)(2,1)S(1)} %pad_maximum_fusion), channel_id=1, source_target_pairs={{0,192},{8,56},{16,208},{24,8},{32,224},{40,24},{48,240},{56,40},{... | collective-permute-start | bytes 442376 | tf_op jit(solution)/shard_map/ppermute | solution.py:295
  21.6 8.3 %collective-permute-start.4 = (bf16[4,144,128]{2,1,0:T(8,128)(2,1)S(1)}, bf16[4,144,128]{2,1,0:T(8,128)(2,1)S(1)}, u32[]{:S(2)}, u32[]{:S(2)}) collective-permute-start(bf16[4,144,128]{2,1,0:T(8,128)(2,1)S(1)} %pad_maximum_fusion), channel_id=1, source_target_pairs={{0,128},{8,40},{16,144},{24,56},{32,160},{40,8},{48,176},{56,24},{... | collective-permute-start | bytes 442376 | tf_op jit(solution)/shard_map/ppermute | solution.py:295
  22.2 7.6 %collective-permute-start.3 = (bf16[4,144,128]{2,1,0:T(8,128)(2,1)S(1)}, bf16[4,144,128]{2,1,0:T(8,128)(2,1)S(1)}, u32[]{:S(2)}, u32[]{:S(2)}) collective-permute-start(bf16[4,144,128]{2,1,0:T(8,128)(2,1)S(1)} %pad_maximum_fusion), channel_id=1, source_target_pairs={{0,64},{8,24},{16,80},{24,40},{32,96},{40,56},{48,112},{56,8},{64,... | collective-permute-start | bytes 442376 | tf_op jit(solution)/shard_map/ppermute | solution.py:295
  29.9 2.1 %collective-permute-start.6 = (bf16[16,144,128]{2,1,0:T(8,128)(2,1)S(1)}, bf16[16,144,128]{2,1,0:T(8,128)(2,1)S(1)}, u32[]{:S(2)}, u32[]{:S(2)}) collective-permute-start(bf16[16,144,128]{2,1,0:T(8,128)(2,1)S(1)} %constant_dynamic-update-slice_fusion.own_ref), channel_id=1, source_target_pairs={{0,8},{8,0},{1,9},{9,1},{2,10},{10,2},{3,11},{11,3},{4,12},{12,4},... | collective-permute-start | bytes 1769480 | tf_op jit(solution)/shard_map/ppermute | solution.py:299
  36.3 0.7 copy-start.6
  43.2 23.6 %all-to-all-start.1 = ((bf16[8,272,128]{2,1,0:T(8,128)(2,1)}), bf16[8,272,128]{2,1,0:T(8,128)(2,1)S(1)}, u32[]{:S(2)}, u32[]{:S(2)}) async-start(bf16[8,272,128]{2,1,0:T(8,128)(2,1)} %get-tuple-element.37), calls=%async_computation.1 | async-start | bytes 1114112 | tf_op jit(solution)/shard_map/all_to_all | solution.py:325
  48.7 2.0 %collective-permute-start.7 = (bf16[16,144,128]{2,1,0:T(8,128)(2,1)S(1)}, bf16[16,144,128]{2,1,0:T(8,128)(2,1)S(1)}, u32[]{:S(2)}, u32[]{:S(2)}) collective-permute-start(bf16[16,144,128]{2,1,0:T(8,128)(2,1)S(1)} %get-tuple-element.29), channel_id=1, source_target_pairs={{0,8},{8,0},{1,9},{9,1},{2,10},{10,2},{3,11},{11,3},{4,12},{12,4},... | collective-permute-start | bytes 1769480 | tf_op jit(solution)/shard_map/ppermute | solution.py:299
  50.9 6.1 %collective-permute-start.8 = (bf16[4,144,128]{2,1,0:T(8,128)(2,1)S(1)}, bf16[4,144,128]{2,1,0:T(8,128)(2,1)S(1)}, u32[]{:S(2)}, u32[]{:S(2)}) collective-permute-start(bf16[4,144,128]{2,1,0:T(8,128)(2,1)S(1)} %get-tuple-element.31), channel_id=1, source_target_pairs={{0,16},{8,72},{16,32},{24,88},{32,48},{40,104},{48,0},{56,120},{64... | collective-permute-start | bytes 442376 | tf_op jit(solution)/shard_map/ppermute | solution.py:295
  52.7 6.8 %collective-permute-start.9 = (bf16[4,144,128]{2,1,0:T(8,128)(2,1)S(1)}, bf16[4,144,128]{2,1,0:T(8,128)(2,1)S(1)}, u32[]{:S(2)}, u32[]{:S(2)}) collective-permute-start(bf16[4,144,128]{2,1,0:T(8,128)(2,1)S(1)} %get-tuple-element.32), channel_id=1, source_target_pairs={{0,32},{8,136},{16,48},{24,152},{32,0},{40,168},{48,16},{56,184},{... | collective-permute-start | bytes 442376 | tf_op jit(solution)/shard_map/ppermute | solution.py:295
  53.2 7.8 %collective-permute-start.10 = (bf16[4,144,128]{2,1,0:T(8,128)(2,1)S(1)}, bf16[4,144,128]{2,1,0:T(8,128)(2,1)S(1)}, u32[]{:S(2)}, u32[]{:S(2)}) collective-permute-start(bf16[4,144,128]{2,1,0:T(8,128)(2,1)S(1)} %get-tuple-element.33), channel_id=1, source_target_pairs={{0,48},{8,200},{16,0},{24,216},{32,16},{40,232},{48,32},{56,248},{... | collective-permute-start | bytes 442376 | tf_op jit(solution)/shard_map/ppermute | solution.py:295
  61.1 7.6 %collective-permute-start.11 = (bf16[144,128]{1,0:T(8,128)(2,1)S(1)}, bf16[144,128]{1,0:T(8,128)(2,1)S(1)}, u32[]{:S(2)}, u32[]{:S(2)}) collective-permute-start(bf16[144,128]{1,0:T(8,128)(2,1)S(1)} %get-tuple-element.34), channel_id=1, source_target_pairs={{0,64},{8,24},{16,80},{24,40},{32,96},{40,56},{48,112},{56,8},{64,... | collective-permute-start | bytes 110600 | tf_op jit(solution)/shard_map/ppermute | solution.py:295
  64.0 5.5 %collective-permute-start.12 = (bf16[144,128]{1,0:T(8,128)(2,1)S(1)}, bf16[144,128]{1,0:T(8,128)(2,1)S(1)}, u32[]{:S(2)}, u32[]{:S(2)}) collective-permute-start(bf16[144,128]{1,0:T(8,128)(2,1)S(1)} %get-tuple-element.35), channel_id=1, source_target_pairs={{0,128},{8,40},{16,144},{24,56},{32,160},{40,8},{48,176},{56,24},{... | collective-permute-start | bytes 110600 | tf_op jit(solution)/shard_map/ppermute | solution.py:295
  64.0 5.5 %collective-permute-start.13 = (bf16[144,128]{1,0:T(8,128)(2,1)S(1)}, bf16[144,128]{1,0:T(8,128)(2,1)S(1)}, u32[]{:S(2)}, u32[]{:S(2)}) collective-permute-start(bf16[144,128]{1,0:T(8,128)(2,1)S(1)} %get-tuple-element.36), channel_id=1, source_target_pairs={{0,192},{8,56},{16,208},{24,8},{32,224},{40,24},{48,240},{56,40},{... | collective-permute-start | bytes 110600 | tf_op jit(solution)/shard_map/ppermute | solution.py:295
